TPU v7x, 32 devices: a whole 2x2x4 slice. The times are simulated.
32 devices in a mesh: face: 2 (over x), px: 4 (over y, core), py: 4 (over z).
Axes of the slice: x: 2, y: 2, z: 4, core: 2. Of those that a mesh axis runs over, the one named last changes fastest.
Arguments:
- tracer_mass: float32 [40, 128, 512], P(None, ('face', 'px'), 'py'), may hold values from -6 to 6
- recon_table: float32 [10, 25], replicated, may hold values from -1.25 to 1.25
- intersection_weights: float32 [4, 10, 128, 512], P(None, None, ('face', 'px'), 'py'), may hold values from -1 to 1
- intersection_cells: int32 [4, 128, 512], P(None, ('face', 'px'), 'py'), may hold values from 0 to 8
- rotation_codes: int32 [4, 128, 512], P(None, ('face', 'px'), 'py'), may hold values from 0 to 3
Outputs:
- advected: float32 [40, 128, 512], P(None, ('face', 'px'), 'py')
Inputs may be any that keep to these rules, and one draw needn't show every extreme that they name: `intersection_cells`: the index of the 3 x 3 neighbour, row-major from offset (-1, -1). `rotation_codes`: a count of quarter turns.
All inputs are finite; a program needn't handle non-finite values.
Results may differ from a plain program's by a relative error of at most 0.0001.
Values sent between devices are 32-bit elements; how exact they have to be, the bound alone decides.
No kernel may reach another device: no remote copies, remote signals or barrier semaphores. Data moves between devices by JAX's collectives and lax.ppermute only.
A program may use at most 256 MiB of HBM per device.

v0:
```python
import jax
import jax.numpy as jnp
import numpy as np
from jax import lax
from jax.sharding import PartitionSpec as P

STEPS = 2


def padded(block, sides, width):
    for axis, dim in sides:
        count = lax.axis_size(axis)
        forward = [(i, i + 1) for i in range(count - 1)]
        backward = [(target, source) for source, target in forward]
        low = lax.ppermute(
            lax.slice_in_dim(block, block.shape[dim] - width, None, axis=dim), axis, forward
        )
        high = lax.ppermute(lax.slice_in_dim(block, 0, width, axis=dim), axis, backward)
        block = jnp.concatenate([low, block, high], axis=dim)
    return block


def rotation_tables():
    exponents = [(0, 0), (1, 0), (0, 1), (2, 0), (1, 1), (0, 2), (3, 0), (2, 1), (1, 2), (0, 3)]
    quarter = np.zeros((10, 10))
    for place, powers in enumerate(exponents):
        target = exponents.index((powers[1], powers[0]))
        quarter[target, place] = (-1.0) ** powers[1]
    tables = [np.eye(10)]
    for turn in range(3):
        tables.append(quarter @ tables[-1])
    return np.stack(tables)


def neighbour_weights(intersection_weights, intersection_cells, rotation_codes):
    tables = jnp.asarray(rotation_tables(), dtype=jnp.float32)
    rotated = jnp.zeros_like(intersection_weights)
    for turn in range(4):
        picked = (rotation_codes == turn).astype(jnp.float32)[:, None]
        turned = jnp.einsum(
            "kl,mkxy->mlxy", tables[turn], intersection_weights, precision=lax.Precision.HIGHEST
        )
        rotated = rotated + picked * turned
    choose = (
        intersection_cells[:, None] == jnp.arange(9, dtype=jnp.int32)[None, :, None, None]
    ).astype(jnp.float32)
    return jnp.einsum("mnxy,mlxy->nlxy", choose, rotated, precision=lax.Precision.HIGHEST)


def combine_stencil(weights, recon_table):
    spread = jnp.einsum("nlxy,lj->njxy", weights, recon_table, precision=lax.Precision.HIGHEST)
    parts = [jnp.zeros(weights.shape[2:], jnp.float32) for offset in range(49)]
    for near in range(9):
        for tap in range(25):
            offset = (near // 3 + tap // 5) * 7 + near % 3 + tap % 5
            parts[offset] = parts[offset] + spread[near, tap]
    return jnp.stack(parts)


def extend(field):
    return padded(field, ((("face", "px"), 1), ("py", 2)), 3)


def apply_step(source, stencil, out_x, out_y):
    stacks = source.shape[0]
    total = jnp.zeros((stacks, out_x, out_y), jnp.float32)
    for offset in range(49):
        shift_x = offset // 7
        shift_y = offset % 7
        total = (
            total
            + stencil[offset][None]
            * source[:, shift_x : shift_x + out_x, shift_y : shift_y + out_y]
        )
    return total


def local(tracer_mass, recon_table, intersection_weights, intersection_cells, rotation_codes):
    stacks, width_x, width_y = tracer_mass.shape
    weights = neighbour_weights(intersection_weights, intersection_cells, rotation_codes)
    field = tracer_mass
    stencil = None
    stencil = combine_stencil(weights, recon_table)
    for step in range(STEPS):
        field = apply_step(extend(field), stencil, width_x, width_y)
    return field


def solution(mesh):
    in_specs = (
        P(None, ("face", "px"), "py"),
        P(),
        P(None, None, ("face", "px"), "py"),
        P(None, ("face", "px"), "py"),
        P(None, ("face", "px"), "py"),
    )
    out_specs = P(None, ("face", "px"), "py")
    return jax.shard_map(local, mesh=mesh, in_specs=in_specs, out_specs=out_specs, check_vma=False)
```

profile of v0, /device:TPU:12, one launch (start us, length us, event | category | flops | bytes accessed | tf_op | source)
XLA Modules:
  0.0 99.7 jit_solution(7786553515600549218)
XLA Ops:
  0.0 0.0 copy-start
  0.0 0.0 copy-start.5
  0.0 0.0 copy-start.4
  0.0 1.1 %fusion.128 = (f32[40,3,128]{2,1,0:T(4,128)S(1)}, f32[40,3,128]{2,1,0:T(4,128)S(1)}) fusion(f32[40,16,128]{2,1,0:T(8,128)} %param.6), kind=kLoop, calls=%fused_computation.424 | loop fusion | bytes 245760 | tf_op jit(solution)/shard_map/slice | solution.py:16
  1.1 1.9 %collective-permute-start = (f32[40,3,128]{2,1,0:T(4,128)S(1)}, f32[40,3,128]{2,1,0:T(4,128)S(1)}, u32[]{:S(2)}, u32[]{:S(2)}) collective-permute-start(f32[40,3,128]{2,1,0:T(4,128)S(1)} %get-tuple-element.63), channel_id=1, source_target_pairs={{0,4},{4,8},{8,12},{12,16},{16,20},{20,24},{24,28},{1,5},{5,9},{9,... | collective-permute-start | bytes 184328 | tf_op jit(solution)/shard_map/ppermute | solution.py:15
  3.0 3.6 %collective-permute-start.1 = (f32[40,3,128]{2,1,0:T(4,128)S(1)}, f32[40,3,128]{2,1,0:T(4,128)S(1)}, u32[]{:S(2)}, u32[]{:S(2)}) collective-permute-start(f32[40,3,128]{2,1,0:T(4,128)S(1)} %get-tuple-element.64), channel_id=1, source_target_pairs={{4,0},{8,4},{12,8},{16,12},{20,16},{24,20},{28,24},{5,1},{9,5},{13... | collective-permute-start | bytes 184328 | tf_op jit(solution)/shard_map/ppermute | solution.py:18
  6.7 0.8 compare_convert_fusion.3
  7.4 0.0 copy-done
  7.5 1.3 %fusion.1 = f32[10,4,16,128]{3,0,2,1:T(8,128)S(1)} fusion(f32[10,10,1,1]{1,0,3,2:T(8,128)} %constant.22, f32[4,10,16,128]{3,2,1,0:T(8,128)S(1)} %copy-done), kind=kOutput, calls=%fused_computation.6 | convolution fusion | flops 9830400 | bytes 655760 | tf_op jit(solution)/shard_map/kl,mkxy->mlxy/dot_general | solution.py:40
  8.8 1.3 %fusion.3 = f32[10,4,16,128]{3,0,2,1:T(8,128)S(1)} fusion(f32[10,10,1,1]{1,0,3,2:T(8,128)} %constant.21, f32[4,10,16,128]{3,2,1,0:T(8,128)S(1)} %copy-done), kind=kOutput, calls=%fused_computation.8 | convolution fusion | flops 9830400 | bytes 655760 | tf_op jit(solution)/shard_map/kl,mkxy->mlxy/dot_general | solution.py:40
  10.1 0.0 copy-done.5
  10.2 0.6 fusion.5
  10.8 0.0 copy-done.4
  10.8 0.6 fusion.7
  11.5 0.4 fusion.120
  11.8 0.0 copy-start.2
  11.9 2.7 %copy.16 = f32[10,4,16,128]{0,1,3,2:T(4,128)} copy(f32[10,4,16,128]{3,2,1,0:T(8,128)S(1)} %fusion.120) | data formatting | bytes 655360 | tf_op jit(solution)/shard_map/add | solution.py:43
  14.5 0.0 copy-done.2
  14.6 1.7 %copy.17 = pred[4,9,16,128]{1,0,3,2:T(4,128)(4,1)S(1)} copy(pred[4,9,16,128]{3,2,1,0:T(8,128)(4,1)S(1)} %iota_compare_fusion) | data formatting | bytes 147456 | tf_op jit(solution)/shard_map/eq | solution.py:45
  16.3 17.1 %fusion.129 = f32[16,128,10,9]{2,3,1,0:T(8,128)} fusion(f32[10,4,16,128]{0,1,3,2:T(4,128)} %copy.16, pred[4,9,16,128]{1,0,3,2:T(4,128)(4,1)S(1)} %copy.17), kind=kOutput, calls=%fused_computation.425 | convolution fusion | flops 8847360 | bytes 1138688 | tf_op jit(solution)/shard_map/mnxy,mlxy->nlxy/dot_general | solution.py:47
  33.4 0.0 copy-start.3
  33.4 9.8 %copy.18 = f32[16,128,10,9]{1,2,0,3:T(8,128)S(1)} copy(f32[16,128,10,9]{2,3,1,0:T(8,128)} %fusion.129) | data formatting | bytes 1474560 | tf_op jit(solution)/shard_map/mnxy,mlxy->nlxy/dot_general | solution.py:47
  43.2 0.0 copy-done.3
  43.2 0.0 copy-start.1
  43.2 2.0 %convolution_bitcast_fusion = f32[9,25,16,128]{3,1,2,0:T(8,128)S(1)} fusion(f32[16,128,10,9]{1,2,0,3:T(8,128)S(1)} %copy.18, f32[10,25]{1,0:T(8,128)S(1)} %copy-done.3), kind=kOutput, calls=%fused_computation | convolution fusion | flops 55296000 | bytes 2581480 | tf_op jit(solution)/shard_map/nlxy,lj->njxy/dot_general | solution.py:51
  45.3 0.1 fusion.124
  45.4 0.1 slice_add_fusion.175
  45.5 0.1 slice_add_fusion.173
  45.6 0.1 slice_add_fusion.138
  45.7 0.1 slice_add_fusion.171
  45.8 0.1 slice_add_fusion.168
  45.9 0.1 slice_add_fusion.169
  46.1 0.1 slice_add_fusion.167
  46.2 0.1 slice_add_fusion.164
  46.3 0.1 slice_add_fusion.130
  46.4 0.1 slice_add_fusion.109
  46.5 0.1 slice_add_fusion.84
  46.6 0.0 copy-done.1
  46.7 0.0 collective-permute-done
  46.7 0.0 collective-permute-done.1
  46.7 0.1 pad_maximum_fusion.2
  46.8 0.2 fusion.126
  47.0 3.5 %collective-permute-start.2 = (f32[40,22,3]{2,1,0:T(8,128)S(1)}, f32[40,22,3]{2,1,0:T(8,128)S(1)}, u32[]{:S(2)}, u32[]{:S(2)}) collective-permute-start(f32[40,22,3]{2,1,0:T(8,128)S(1)} %get-tuple-element.59), channel_id=1, source_target_pairs={{0,1},{1,2},{2,3},{4,5},{5,6},{6,7},{8,9},{9,10},{10,11},{12,13},{... | collective-permute-start | bytes 31688 | tf_op jit(solution)/shard_map/ppermute | solution.py:15
  50.5 2.6 %collective-permute-start.3 = (f32[40,22,3]{2,1,0:T(8,128)S(1)}, f32[40,22,3]{2,1,0:T(8,128)S(1)}, u32[]{:S(2)}, u32[]{:S(2)}) collective-permute-start(f32[40,22,3]{2,1,0:T(8,128)S(1)} %get-tuple-element.60), channel_id=1, source_target_pairs={{1,0},{2,1},{3,2},{5,4},{6,5},{7,6},{9,8},{10,9},{11,10},{13,12},{... | collective-permute-start | bytes 31688 | tf_op jit(solution)/shard_map/ppermute | solution.py:18
  53.1 8.7 %collective-permute-done.2 = f32[40,22,3]{2,1,0:T(8,128)S(1)} collective-permute-done((f32[40,22,3]{2,1,0:T(8,128)S(1)}, f32[40,22,3]{2,1,0:T(8,128)S(1)}, u32[]{:S(2)}, u32[]{:S(2)}) %collective-permute-start.2) | collective-permute-done | bytes 10592 | tf_op jit(solution)/shard_map/ppermute | solution.py:15
  61.8 3.2 %collective-permute-done.3 = f32[40,22,3]{2,1,0:T(8,128)S(1)} collective-permute-done((f32[40,22,3]{2,1,0:T(8,128)S(1)}, f32[40,22,3]{2,1,0:T(8,128)S(1)}, u32[]{:S(2)}, u32[]{:S(2)}) %collective-permute-start.3) | collective-permute-done | bytes 10592 | tf_op jit(solution)/shard_map/ppermute | solution.py:18
  65.0 0.5 maximum_maximum_fusion
  65.6 3.5 %fusion.99 = f32[40,16,128]{2,1,0:T(8,128)S(1)} fusion(f32[40,22,131]{2,1,0:T(8,128)S(1)} %get-tuple-element.58, f32[40,19,128]{2,1,0:T(8,128)S(1)} %constant_dynamic-update-slice_fusion, f32[40,22,131]{2,1,0:T(8,128)S(1)} %get-tuple-element.57, f32[40,16,128]{2,1,0:T(8,128)S(1)} %copy-done.1, f32[40,3,128]{2,1,0:T(4,128)S(1)} %collective-permute-done, ...), kind=kLoop, calls=%fused_computation.163 | loop fusion | flops 8192000 | bytes 15863808 | tf_op jit(solution)/shard_map/add | solution.py:71
  69.1 1.9 %collective-permute-start.4 = (f32[40,3,128]{2,1,0:T(4,128)S(1)}, f32[40,3,128]{2,1,0:T(4,128)S(1)}, u32[]{:S(2)}, u32[]{:S(2)}) collective-permute-start(f32[40,3,128]{2,1,0:T(4,128)S(1)} %get-tuple-element.61), channel_id=1, source_target_pairs={{0,4},{4,8},{8,12},{12,16},{16,20},{20,24},{24,28},{1,5},{5,9},{9,... | collective-permute-start | bytes 184328 | tf_op jit(solution)/shard_map/ppermute | solution.py:15
  71.0 3.6 %collective-permute-start.5 = (f32[40,3,128]{2,1,0:T(4,128)S(1)}, f32[40,3,128]{2,1,0:T(4,128)S(1)}, u32[]{:S(2)}, u32[]{:S(2)}) collective-permute-start(f32[40,3,128]{2,1,0:T(4,128)S(1)} %get-tuple-element.62), channel_id=1, source_target_pairs={{4,0},{8,4},{12,8},{16,12},{20,16},{24,20},{28,24},{5,1},{9,5},{13... | collective-permute-start | bytes 184328 | tf_op jit(solution)/shard_map/ppermute | solution.py:18
  74.7 0.2 collective-permute-done.4
  74.8 1.9 %collective-permute-done.5 = f32[40,3,128]{2,1,0:T(4,128)S(1)} collective-permute-done((f32[40,3,128]{2,1,0:T(4,128)S(1)}, f32[40,3,128]{2,1,0:T(4,128)S(1)}, u32[]{:S(2)}, u32[]{:S(2)}) %collective-permute-start.5) | collective-permute-done | bytes 61472 | tf_op jit(solution)/shard_map/ppermute | solution.py:18
  76.7 0.1 pad_maximum_fusion.3
  76.8 0.2 fusion.125
  77.0 3.5 %collective-permute-start.6 = (f32[40,22,3]{2,1,0:T(8,128)S(1)}, f32[40,22,3]{2,1,0:T(8,128)S(1)}, u32[]{:S(2)}, u32[]{:S(2)}) collective-permute-start(f32[40,22,3]{2,1,0:T(8,128)S(1)} %get-tuple-element.55), channel_id=1, source_target_pairs={{0,1},{1,2},{2,3},{4,5},{5,6},{6,7},{8,9},{9,10},{10,11},{12,13},{... | collective-permute-start | bytes 31688 | tf_op jit(solution)/shard_map/ppermute | solution.py:15
  80.5 2.4 %collective-permute-start.7 = (f32[40,22,3]{2,1,0:T(8,128)S(1)}, f32[40,22,3]{2,1,0:T(8,128)S(1)}, u32[]{:S(2)}, u32[]{:S(2)}) collective-permute-start(f32[40,22,3]{2,1,0:T(8,128)S(1)} %get-tuple-element.56), channel_id=1, source_target_pairs={{1,0},{2,1},{3,2},{5,4},{6,5},{7,6},{9,8},{10,9},{11,10},{13,12},{... | collective-permute-start | bytes 31688 | tf_op jit(solution)/shard_map/ppermute | solution.py:18
  82.9 8.4 %collective-permute-done.6 = f32[40,22,3]{2,1,0:T(8,128)S(1)} collective-permute-done((f32[40,22,3]{2,1,0:T(8,128)S(1)}, f32[40,22,3]{2,1,0:T(8,128)S(1)}, u32[]{:S(2)}, u32[]{:S(2)}) %collective-permute-start.6) | collective-permute-done | bytes 10592 | tf_op jit(solution)/shard_map/ppermute | solution.py:15
  91.3 3.8 %collective-permute-done.7 = f32[40,22,3]{2,1,0:T(8,128)S(1)} collective-permute-done((f32[40,22,3]{2,1,0:T(8,128)S(1)}, f32[40,22,3]{2,1,0:T(8,128)S(1)}, u32[]{:S(2)}, u32[]{:S(2)}) %collective-permute-start.7) | collective-permute-done | bytes 10592 | tf_op jit(solution)/shard_map/ppermute | solution.py:18
  95.1 0.5 maximum_maximum_fusion.1
  95.6 4.1 %fusion.21 = f32[40,16,128]{2,1,0:T(8,128)} fusion(f32[40,16,128]{2,1,0:T(8,128)S(1)} %fusion.99, f32[40,3,128]{2,1,0:T(4,128)S(1)} %collective-permute-done.5, f32[40,3,128]{2,1,0:T(4,128)S(1)} %collective-permute-done.4, f32[40,22,131]{2,1,0:T(8,128)S(1)} %get-tuple-element.54, f32[40,22,131]{2,1,0:T(8,128)S(1)} %get-tuple-element.53, ...), kind=kLoop, calls=%fused_computation.40 | loop fusion | flops 8437760 | bytes 14942208 | tf_op jit(solution)/shard_map/add | solution.py:71
  (5 shorter events, 0.2 us)
Async XLA Ops:
  0.0 7.4 %copy-start = (f32[4,10,16,128]{3,2,1,0:T(8,128)S(1)}, f32[4,10,16,128]{3,2,1,0:T(8,128)}, u32[]{:S(2)}) copy-start(f32[4,10,16,128]{3,2,1,0:T(8,128)} %param.8) | copy-start | bytes 983044
  0.0 10.1 %copy-start.5 = (f32[10,10,1,1]{1,0,3,2:T(8,128)S(1)}, f32[10,10,1,1]{1,0,3,2:T(8,128)}, u32[]{:S(2)}) copy-start(f32[10,10,1,1]{1,0,3,2:T(8,128)} %constant.20) | copy-start | bytes 1204
  0.0 10.8 %copy-start.4 = (f32[10,10,1,1]{1,0,3,2:T(8,128)S(1)}, f32[10,10,1,1]{1,0,3,2:T(8,128)}, u32[]{:S(2)}) copy-start(f32[10,10,1,1]{1,0,3,2:T(8,128)} %constant.19) | copy-start | bytes 1204
  1.1 45.6 %collective-permute-start = (f32[40,3,128]{2,1,0:T(4,128)S(1)}, f32[40,3,128]{2,1,0:T(4,128)S(1)}, u32[]{:S(2)}, u32[]{:S(2)}) collective-permute-start(f32[40,3,128]{2,1,0:T(4,128)S(1)} %get-tuple-element.63), channel_id=1, source_target_pairs={{0,4},{4,8},{8,12},{12,16},{16,20},{20,24},{24,28},{1,5},{5,9},{9,... | collective-permute-start | bytes 184328 | tf_op jit(solution)/shard_map/ppermute | solution.py:15
  3.0 43.7 %collective-permute-start.1 = (f32[40,3,128]{2,1,0:T(4,128)S(1)}, f32[40,3,128]{2,1,0:T(4,128)S(1)}, u32[]{:S(2)}, u32[]{:S(2)}) collective-permute-start(f32[40,3,128]{2,1,0:T(4,128)S(1)} %get-tuple-element.64), channel_id=1, source_target_pairs={{4,0},{8,4},{12,8},{16,12},{20,16},{24,20},{28,24},{5,1},{9,5},{13... | collective-permute-start | bytes 184328 | tf_op jit(solution)/shard_map/ppermute | solution.py:18
  11.8 2.7 %copy-start.2 = (s32[4,16,128]{2,1,0:T(8,128)S(1)}, s32[4,16,128]{2,1,0:T(8,128)}, u32[]{:S(2)}) copy-start(s32[4,16,128]{2,1,0:T(8,128)} %param.9) | copy-start | bytes 98308
  33.4 9.8 %copy-start.3 = (f32[10,25]{1,0:T(8,128)S(1)}, f32[10,25]{1,0:T(8,128)}, u32[]{:S(2)}) copy-start(f32[10,25]{1,0:T(8,128)} %param.7) | copy-start | bytes 3004
  43.2 3.4 %copy-start.1 = (f32[40,16,128]{2,1,0:T(8,128)S(1)}, f32[40,16,128]{2,1,0:T(8,128)}, u32[]{:S(2)}) copy-start(f32[40,16,128]{2,1,0:T(8,128)} %param.6) | copy-start | bytes 983044
  47.0 14.8 %collective-permute-start.2 = (f32[40,22,3]{2,1,0:T(8,128)S(1)}, f32[40,22,3]{2,1,0:T(8,128)S(1)}, u32[]{:S(2)}, u32[]{:S(2)}) collective-permute-start(f32[40,22,3]{2,1,0:T(8,128)S(1)} %get-tuple-element.59), channel_id=1, source_target_pairs={{0,1},{1,2},{2,3},{4,5},{5,6},{6,7},{8,9},{9,10},{10,11},{12,13},{... | collective-permute-start | bytes 31688 | tf_op jit(solution)/shard_map/ppermute | solution.py:15
  50.5 14.6 %collective-permute-start.3 = (f32[40,22,3]{2,1,0:T(8,128)S(1)}, f32[40,22,3]{2,1,0:T(8,128)S(1)}, u32[]{:S(2)}, u32[]{:S(2)}) collective-permute-start(f32[40,22,3]{2,1,0:T(8,128)S(1)} %get-tuple-element.60), channel_id=1, source_target_pairs={{1,0},{2,1},{3,2},{5,4},{6,5},{7,6},{9,8},{10,9},{11,10},{13,12},{... | collective-permute-start | bytes 31688 | tf_op jit(solution)/shard_map/ppermute | solution.py:18
  69.1 5.8 %collective-permute-start.4 = (f32[40,3,128]{2,1,0:T(4,128)S(1)}, f32[40,3,128]{2,1,0:T(4,128)S(1)}, u32[]{:S(2)}, u32[]{:S(2)}) collective-permute-start(f32[40,3,128]{2,1,0:T(4,128)S(1)} %get-tuple-element.61), channel_id=1, source_target_pairs={{0,4},{4,8},{8,12},{12,16},{16,20},{20,24},{24,28},{1,5},{5,9},{9,... | collective-permute-start | bytes 184328 | tf_op jit(solution)/shard_map/ppermute | solution.py:15
  71.0 5.7 %collective-permute-start.5 = (f32[40,3,128]{2,1,0:T(4,128)S(1)}, f32[40,3,128]{2,1,0:T(4,128)S(1)}, u32[]{:S(2)}, u32[]{:S(2)}) collective-permute-start(f32[40,3,128]{2,1,0:T(4,128)S(1)} %get-tuple-element.62), channel_id=1, source_target_pairs={{4,0},{8,4},{12,8},{16,12},{20,16},{24,20},{28,24},{5,1},{9,5},{13... | collective-permute-start | bytes 184328 | tf_op jit(solution)/shard_map/ppermute | solution.py:18
  77.0 14.3 %collective-permute-start.6 = (f32[40,22,3]{2,1,0:T(8,128)S(1)}, f32[40,22,3]{2,1,0:T(8,128)S(1)}, u32[]{:S(2)}, u32[]{:S(2)}) collective-permute-start(f32[40,22,3]{2,1,0:T(8,128)S(1)} %get-tuple-element.55), channel_id=1, source_target_pairs={{0,1},{1,2},{2,3},{4,5},{5,6},{6,7},{8,9},{9,10},{10,11},{12,13},{... | collective-permute-start | bytes 31688 | tf_op jit(solution)/shard_map/ppermute | solution.py:15
  80.5 14.6 %collective-permute-start.7 = (f32[40,22,3]{2,1,0:T(8,128)S(1)}, f32[40,22,3]{2,1,0:T(8,128)S(1)}, u32[]{:S(2)}, u32[]{:S(2)}) collective-permute-start(f32[40,22,3]{2,1,0:T(8,128)S(1)} %get-tuple-element.56), channel_id=1, source_target_pairs={{1,0},{2,1},{3,2},{5,4},{6,5},{7,6},{9,8},{10,9},{11,10},{13,12},{... | collective-permute-start | bytes 31688 | tf_op jit(solution)/shard_map/ppermute | solution.py:18
where the time goes:
time: 102 us; the launch traced here: 99.7 us
  waiting for transfers between devices  26.2 us (26%)
  matrix products  23.1 us (23%)
  starting transfers between devices  23 us (23%)
  local copies, waits for them, and re-layouts  15.8 us (15%)
  other arithmetic  11.3 us (11%)
    ppermute x4, waiting for transfers between devices, padded(): lax.ppermute(lax.slice_in_dim(block, block.shape[dim] - width, None, axis...  17.3 us
    dot_general x1, matrix products, neighbour_weights(): jnp.einsum('mnxy,mlxy->nlxy', choose, rotated, precision=lax.Precision.HI...  17.1 us
    ppermute x4, starting transfers between devices, padded(): lax.ppermute(lax.slice_in_dim(block, 0, width, axis=dim), axis, backward)  12.2 us
    ppermute x4, starting transfers between devices, padded(): lax.ppermute(lax.slice_in_dim(block, block.shape[dim] - width, None, axis...  10.8 us
    dot_general x1, local copies, waits for them, and re-layouts, neighbour_weights(): jnp.einsum('mnxy,mlxy->nlxy', choose, rotated, precision=lax.Precision.HI...  9.81 us
    ppermute x4, waiting for transfers between devices, padded(): lax.ppermute(lax.slice_in_dim(block, 0, width, axis=dim), axis, backward)  8.86 us
    add x2, other arithmetic, apply_step(): total + stencil[offset][None] * source[:, shift_x:shift_x + out_x, shift_...  7.59 us
    dot_general x4, matrix products, neighbour_weights(): jnp.einsum('kl,mkxy->mlxy', tables[turn], intersection_weights, precision...  3.96 us
  transfers between devices with their start and end apart: 8, of which 6 were waited for; matrix products, arithmetic and copies ran while one was open for 40% of the time, Pallas kernels for 0%

commit v1 on v0

v1 whole, which is shorter than its diff:
```python
import functools

import jax
import jax.numpy as jnp
from jax import lax
from jax.experimental import pallas as pl
from jax.experimental.pallas import tpu as pltpu
from jax.sharding import PartitionSpec as P

F32 = jnp.float32
SWAPPED = (0, 2, 1, 5, 4, 3, 9, 8, 7, 6)
POWERS = ((0, 0), (1, 0), (0, 1), (2, 0), (1, 1), (0, 2), (3, 0), (2, 1), (1, 2), (0, 3))
TERMS = 10
GROUP = 4
VMEM = pl.BlockSpec(memory_space=pltpu.VMEM)
SMEM = pl.BlockSpec(memory_space=pltpu.SMEM)
PARAMS = pltpu.CompilerParams(vmem_limit_bytes=40 * 1024 * 1024)


def swap(block, axes, odd_first):
    count = lax.axis_size(axes)
    pairs = []
    for low in range(1 if odd_first else 0, count - 1, 2):
        pairs += [(low, low + 1), (low + 1, low)]
    return lax.ppermute(block, axes, pairs)


def fill_stencil(recon, weights, cells, codes, turned, spread, stencil, tiles):
    zero = jnp.zeros((8, 128), F32)
    for g in range(tiles):
        rows = pl.ds(8 * g, 8)
        for m in range(4):
            code = codes[m, rows, :]
            odd = (code & 1) == 1
            sign_x = jnp.where(code >= 2, -1.0, 1.0).astype(F32)
            sign_y = jnp.where((code == 1) | (code == 2), -1.0, 1.0).astype(F32)
            sign_xy = sign_x * sign_y
            values = [weights[m, t, rows, :] for t in range(TERMS)]
            for t, (a, b) in enumerate(POWERS):
                value = values[t]
                if SWAPPED[t] != t:
                    value = jnp.where(odd, values[SWAPPED[t]], value)
                if a % 2 and b % 2:
                    value = value * sign_xy
                elif a % 2:
                    value = value * sign_x
                elif b % 2:
                    value = value * sign_y
                turned[t, m * tiles + g] = value

    combos = 4 * tiles

    def one_tap(tap, carry):
        total = [None] * combos
        for t in range(TERMS):
            scale = recon[t, tap]
            for c in range(combos):
                term = turned[t, c] * scale
                total[c] = term if t == 0 else total[c] + term
        for c in range(combos):
            spread[tap, c] = total[c]
        return carry

    lax.fori_loop(0, 25, one_tap, 0)

    for g in range(tiles):
        rows = pl.ds(8 * g, 8)
        masks = []
        for m in range(4):
            cell = cells[m, rows, :]
            first = jnp.where(cell < 3, 0, jnp.where(cell < 6, 3, 6))
            across = cell - first
            masks.append((cell < 3, cell < 6, across == 0, across <= 1))
        for ox in range(7):
            total = [None] * 7
            for m in range(4):
                low_x, mid_x, low_y, mid_y = masks[m]

                def tap(jx, jy):
                    if 0 <= jx < 5 and 0 <= jy < 5:
                        return spread[jx * 5 + jy, m * tiles + g]
                    return zero

                line = [
                    jnp.where(low_x, tap(ox, jy), jnp.where(mid_x, tap(ox - 1, jy), tap(ox - 2, jy)))
                    for jy in range(5)
                ]
                padded = [zero, zero] + line + [zero, zero]
                for oy in range(7):
                    value = jnp.where(
                        low_y, padded[oy + 2], jnp.where(mid_y, padded[oy + 1], padded[oy])
                    )
                    total[oy] = value if m == 0 else total[oy] + value
            for oy in range(7):
                stencil[ox * 7 + oy, rows, :] = total[oy]


def first_kernel(parity, recon, mass, weights, cells, codes, stencil, send_a, send_b, turned, spread):
    fill_stencil(recon, weights, cells, codes, turned, spread, stencil, 2)
    stacks, width = mass.shape[:2]
    even = parity[0] == 0
    for send, low_edge in ((send_a, jnp.logical_not(even)), (send_b, even)):
        mass_at = jnp.where(low_edge, 0, width - 6)
        stencil_at = jnp.where(low_edge, 0, width - 3)
        for s in range(stacks):
            send[6 * s : 6 * s + 6, :] = mass[s, pl.ds(mass_at, 6), :]
        for o in range(49):
            at = 6 * stacks + 3 * o
            send[at : at + 3, :] = stencil[o, pl.ds(stencil_at, 3), :]


def pack_columns(field, tiles, even, send_a, send_b):
    stacks = field.shape[0]
    lane = lax.broadcasted_iota(jnp.int32, (8, 128), 1)
    for tile in range(tiles):
        rows = pl.ds(8 * tile, 8)
        left = jnp.zeros((8, 128), F32)
        right = jnp.zeros((8, 128), F32)
        for s in range(stacks):
            here = (lane >= 3 * s) & (lane < 3 * s + 3)
            value = field[s, rows, :]
            left = jnp.where(here, pltpu.roll(value, (3 * s) % 128, 1), left)
            right = jnp.where(here, pltpu.roll(value, (3 * s - 125) % 128, 1), right)
        send_a[rows, :] = jnp.where(even, right, left)
        send_b[rows, :] = jnp.where(even, left, right)


def second_kernel(parity, mass, stencil, got_a, got_b, field, wide, send_a, send_b):
    stacks, width = mass.shape[:2]
    even = parity[0] == 0

    def place(above, below):
        for s in range(stacks):
            field[s, 0:6, :] = above[6 * s : 6 * s + 6, :]
            field[s, width + 6 : width + 12, :] = below[6 * s : 6 * s + 6, :]
        for o in range(49):
            at = 6 * stacks + 3 * o
            wide[o, 0:3, :] = above[at : at + 3, :]
            wide[o, width + 3 : width + 6, :] = below[at : at + 3, :]

    @pl.when(even)
    def _():
        place(got_b, got_a)

    @pl.when(jnp.logical_not(even))
    def _():
        place(got_a, got_b)

    for s in range(stacks):
        field[s, 6 : width + 6, :] = mass[s, :, :]
        field[s, width + 12 : width + 16, :] = jnp.zeros((4, 128), F32)
    for o in range(49):
        wide[o, 3 : width + 3, :] = stencil[o, :, :]
        wide[o, width + 6 : width + 8, :] = jnp.zeros((2, 128), F32)
    pack_columns(field, 4, parity[1] == 0, send_a, send_b)


def apply_stencil(even, field, stencil, got_a, got_b, out, shifted, in_tiles, out_tiles):
    stacks = field.shape[0]
    lane = lax.broadcasted_iota(jnp.int32, (8, 128), 1)

    def some_stacks(group, carry):
        for k in range(GROUP):
            s = group * GROUP + k
            for tile in range(in_tiles):
                rows = pl.ds(8 * tile, 8)
                one, two = got_a[rows, :], got_b[rows, :]
                after = jnp.where(even, one, two)
                before = jnp.where(even, two, one)
                halo = jnp.where(
                    lane < 64,
                    pltpu.roll(after, lax.rem(128 - 3 * s, 128), 1),
                    pltpu.roll(before, 125 - 3 * s, 1),
                )
                value = field[s, rows, :]
                for dy in range(-3, 4):
                    if dy > 0:
                        moved = pltpu.roll(jnp.where(lane < dy, halo, value), 128 - dy, 1)
                    elif dy < 0:
                        moved = pltpu.roll(jnp.where(lane >= 128 + dy, halo, value), -dy, 1)
                    else:
                        moved = value
                    shifted[k, dy + 3, rows, :] = moved
        for tile in range(out_tiles):
            total = [None] * GROUP
            for dy in range(7):
                for dx in range(7):
                    scale = stencil[dx * 7 + dy, 8 * tile : 8 * tile + 8, :]
                    for k in range(GROUP):
                        at = 8 * tile + dx
                        term = scale * shifted[k, dy, at : at + 8, :]
                        total[k] = term if total[k] is None else total[k] + term
            for k in range(GROUP):
                out[group * GROUP + k, 8 * tile : 8 * tile + 8, :] = total[k]
        return carry

    lax.fori_loop(0, stacks // GROUP, some_stacks, 0)


def third_kernel(parity, field, wide, got_a, got_b, out, send_a, send_b, shifted):
    even = parity[1] == 0
    apply_stencil(even, field, wide, got_a, got_b, out, shifted, 4, 3)
    pack_columns(out, 3, even, send_a, send_b)


def fourth_kernel(parity, field, stencil, got_a, got_b, out, shifted):
    apply_stencil(parity[1] == 0, field, stencil, got_a, got_b, out, shifted, 3, 2)


def local(tracer_mass, recon_table, intersection_weights, intersection_cells, rotation_codes):
    stacks, width_x, width_y = tracer_mass.shape
    row_axes, column_axes = ("face", "px"), "py"
    shape = lambda *sizes: jax.ShapeDtypeStruct(sizes, F32)
    parity = jnp.stack([lax.axis_index(row_axes) % 2, lax.axis_index(column_axes) % 2]).astype(jnp.int32)
    edge = -(-(6 * stacks + 3 * 49) // 8) * 8

    stencil, send_a, send_b = pl.pallas_call(
        first_kernel,
        out_shape=(shape(49, width_x, 128), shape(edge, 128), shape(edge, 128)),
        in_specs=[SMEM, SMEM, VMEM, VMEM, VMEM, VMEM],
        out_specs=(VMEM, VMEM, VMEM),
        scratch_shapes=[pltpu.VMEM((TERMS, 8, 8, 128), F32), pltpu.VMEM((25, 8, 8, 128), F32)],
        compiler_params=PARAMS,
        name="coefficients",
    )(parity, recon_table, tracer_mass, intersection_weights, intersection_cells, rotation_codes)
    got_a = swap(send_a, row_axes, False)
    got_b = swap(send_b, row_axes, True)

    field, wide, send_a, send_b = pl.pallas_call(
        second_kernel,
        out_shape=(shape(stacks, 32, 128), shape(49, 24, 128), shape(32, 128), shape(32, 128)),
        in_specs=[SMEM, VMEM, VMEM, VMEM, VMEM],
        out_specs=(VMEM,) * 4,
        compiler_params=PARAMS,
        name="assemble",
    )(parity, tracer_mass, stencil, got_a, got_b)
    got_a = swap(send_a, column_axes, False)
    got_b = swap(send_b, column_axes, True)

    field, send_a, send_b = pl.pallas_call(
        third_kernel,
        out_shape=(shape(stacks, 24, 128), shape(24, 128), shape(24, 128)),
        in_specs=[SMEM, VMEM, VMEM, VMEM, VMEM],
        out_specs=(VMEM,) * 3,
        scratch_shapes=[pltpu.VMEM((GROUP, 7, 32, 128), F32)],
        compiler_params=PARAMS,
        name="step_one",
    )(parity, field, wide, got_a, got_b)
    got_a = swap(send_a, column_axes, False)
    got_b = swap(send_b, column_axes, True)

    return pl.pallas_call(
        fourth_kernel,
        out_shape=shape(stacks, width_x, 128),
        in_specs=[SMEM, VMEM, VMEM, VMEM, VMEM],
        out_specs=VMEM,
        scratch_shapes=[pltpu.VMEM((GROUP, 7, 24, 128), F32)],
        compiler_params=PARAMS,
        name="step_two",
    )(parity, field, stencil, got_a, got_b)


def solution(mesh):
    in_specs = (
        P(None, ("face", "px"), "py"),
        P(),
        P(None, None, ("face", "px"), "py"),
        P(None, ("face", "px"), "py"),
        P(None, ("face", "px"), "py"),
    )
    out_specs = P(None, ("face", "px"), "py")
    return jax.shard_map(local, mesh=mesh, in_specs=in_specs, out_specs=out_specs, check_vma=False)
```

time: 102 us -> 37.6 us (0.37)
  the two profiles are of different devices: /device:TPU:12 before, /device:TPU:20 now
where the time goes in v1:
time: 37.6 us; the launch traced here: 37.3 us
  waiting for transfers between devices  14 us (37%)
  Pallas kernels  11.7 us (31%)
  starting transfers between devices  8.12 us (22%)
  local copies, waits for them, and re-layouts  3.34 us (9%)
    ppermute x6, waiting for transfers between devices, swap(): return lax.ppermute(block, axes, pairs)  14 us
    ppermute x6, starting transfers between devices, swap(): return lax.ppermute(block, axes, pairs)  8.12 us
    pallas_call x1, Pallas kernels, local(): pl.pallas_call(third_kernel, out_shape=(shape(stacks, 24, 128), shape(24,...  4.84 us
    pallas_call x1, Pallas kernels, local(): pl.pallas_call(fourth_kernel, out_shape=shape(stacks, width_x, 128), in_s...  4.02 us
    unnamed x10, local copies, waits for them, and re-layouts  3.34 us
    pallas_call x1, Pallas kernels, local(): pl.pallas_call(first_kernel, out_shape=(shape(49, width_x, 128), shape(ed...  1.76 us
    pallas_call x1, Pallas kernels, local(): pl.pallas_call(second_kernel, out_shape=(shape(stacks, 32, 128), shape(49...  1.05 us
  transfers between devices with their start and end apart: 6, of which 5 were waited for; matrix products, arithmetic and copies ran while one was open for 0% of the time, Pallas kernels for 0%

profile of v1, /device:TPU:20, one launch (start us, length us, event | category | flops | bytes accessed | tf_op | source)
XLA Modules:
  0.0 37.3 jit_solution(2716254678933621893)
XLA Ops:
  0.0 0.0 copy-start.3
  0.0 0.0 copy-start.2
  0.0 0.1 pad_add_fusion.parity
  0.1 0.7 %copy-done.3 = s32[4,16,128]{2,1,0:T(8,128)S(1)} copy-done((s32[4,16,128]{2,1,0:T(8,128)S(1)}, s32[4,16,128]{2,1,0:T(8,128)}, u32[]{:S(2)}) %copy-start.3) | copy-done | bytes 32792
  0.8 0.0 copy-done.2
  0.8 0.0 copy-start
  0.8 1.0 %copy-done = f32[40,16,128]{2,1,0:T(8,128)S(1)} copy-done((f32[40,16,128]{2,1,0:T(8,128)S(1)}, f32[40,16,128]{2,1,0:T(8,128)}, u32[]{:S(2)}) %copy-start) | copy-done | bytes 327704
  1.7 0.0 copy-start.1
  1.8 1.0 %copy-done.1 = f32[4,10,16,128]{3,2,1,0:T(8,128)S(1)} copy-done((f32[4,10,16,128]{3,2,1,0:T(8,128)S(1)}, f32[4,10,16,128]{3,2,1,0:T(8,128)}, u32[]{:S(2)}) %copy-start.1) | copy-done | bytes 327704
  2.7 0.0 copy-start.4
  2.7 0.7 %copy-done.4 = f32[10,25]{1,0:T(8,128)S(1)} copy-done((f32[10,25]{1,0:T(8,128)S(1)}, f32[10,25]{1,0:T(8,128)}, u32[]{:S(2)}) %copy-start.4) | copy-done | bytes 1024
  3.4 1.8 %coefficients.1 = (f32[49,16,128]{2,1,0:T(8,128)S(1)}, f32[392,128]{1,0:T(8,128)S(1)}, f32[392,128]{1,0:T(8,128)S(1)}) custom-call(s32[2]{0:T(128)S(1)} %pad_add_fusion.parity, f32[10,25]{1,0:T(8,128)S(1)} %copy-done.4, f32[40,16,128]{2,1,0:T(8,128)S(1)} %copy-done, f32[4,10,16,128]{3,2,1,0:T(8,128)S(1)} %copy-done.1, s32[4,16,128]{2,1,0:T(8,128)S(1)} %copy-done.2, ...), custom_call_target="tpu_custom_call" | custom-call | tf_op jit(solution)/shard_map/coefficients/pallas_call | solution.py:217
  5.2 0.1 collective-permute-start
  5.3 2.5 %collective-permute-start.1 = (f32[392,128]{1,0:T(8,128)S(1)}, f32[392,128]{1,0:T(8,128)S(1)}, u32[]{:S(2)}, u32[]{:S(2)}) collective-permute-start(f32[392,128]{1,0:T(8,128)S(1)} %get-tuple-element.17), channel_id=1, source_target_pairs={{4,8},{8,4},{12,16},{16,12},{20,24},{24,20},{5,9},{9,5},{13,17},{1... | collective-permute-start | bytes 602120 | tf_op jit(solution)/shard_map/ppermute | solution.py:25
  7.8 0.0 collective-permute-done.got_a
  7.8 6.7 %collective-permute-done.1.got_b = f32[392,128]{1,0:T(8,128)S(1)} collective-permute-done((f32[392,128]{1,0:T(8,128)S(1)}, f32[392,128]{1,0:T(8,128)S(1)}, u32[]{:S(2)}, u32[]{:S(2)}) %collective-permute-start.1) | collective-permute-done | bytes 200736 | tf_op jit(solution)/shard_map/ppermute | solution.py:25
  14.4 1.0 %assemble.1 = (f32[40,32,128]{2,1,0:T(8,128)S(1)}, f32[49,24,128]{2,1,0:T(8,128)S(1)}, f32[32,128]{1,0:T(8,128)S(1)}, f32[32,128]{1,0:T(8,128)S(1)}) custom-call(s32[2]{0:T(128)S(1)} %pad_add_fusion.parity, f32[40,16,128]{2,1,0:T(8,128)S(1)} %copy-done, f32[49,16,128]{2,1,0:T(8,128)S(1)} %get-tuple-element.15.stencil, ...), custom_call_target="tpu_custom_call" | custom-call | tf_op jit(solution)/shard_map/assemble/pallas_call | solution.py:229
  15.5 1.6 %collective-permute-start.2 = (f32[32,128]{1,0:T(8,128)S(1)}, f32[32,128]{1,0:T(8,128)S(1)}, u32[]{:S(2)}, u32[]{:S(2)}) collective-permute-start(f32[32,128]{1,0:T(8,128)S(1)} %get-tuple-element.20), channel_id=1, source_target_pairs={{0,1},{1,0},{2,3},{3,2},{4,5},{5,4},{6,7},{7,6},{8,9},{9,8},{10,11... | collective-permute-start | bytes 49160 | tf_op jit(solution)/shard_map/ppermute | solution.py:25
  17.1 1.9 %collective-permute-start.3 = (f32[32,128]{1,0:T(8,128)S(1)}, f32[32,128]{1,0:T(8,128)S(1)}, u32[]{:S(2)}, u32[]{:S(2)}) collective-permute-start(f32[32,128]{1,0:T(8,128)S(1)} %get-tuple-element.21), channel_id=1, source_target_pairs={{1,2},{2,1},{5,6},{6,5},{9,10},{10,9},{13,14},{14,13},{17,18},{18,... | collective-permute-start | bytes 49160 | tf_op jit(solution)/shard_map/ppermute | solution.py:25
  19.0 0.2 collective-permute-done.2.got_a
  19.3 3.5 %collective-permute-done.3.got_b = f32[32,128]{1,0:T(8,128)S(1)} collective-permute-done((f32[32,128]{1,0:T(8,128)S(1)}, f32[32,128]{1,0:T(8,128)S(1)}, u32[]{:S(2)}, u32[]{:S(2)}) %collective-permute-start.3) | collective-permute-done | bytes 16416 | tf_op jit(solution)/shard_map/ppermute | solution.py:25
  22.8 4.8 %step_one.1 = (f32[40,24,128]{2,1,0:T(8,128)S(1)}, f32[24,128]{1,0:T(8,128)S(1)}, f32[24,128]{1,0:T(8,128)S(1)}) custom-call(s32[2]{0:T(128)S(1)} %pad_add_fusion.parity, f32[40,32,128]{2,1,0:T(8,128)S(1)} %get-tuple-element.18.field, f32[49,24,128]{2,1,0:T(8,128)S(1)} %get-tuple-element.19.wide, f32[32,128]{1,0:T(8,128)S(1)} %collective-permute-done.2.got_a, ...), custom_call_target="tpu_custom_call" | custom-call | tf_op jit(solution)/shard_map/step_one/pallas_call | solution.py:240
  27.6 0.1 collective-permute-start.4
  27.7 1.9 %collective-permute-start.5 = (f32[24,128]{1,0:T(8,128)S(1)}, f32[24,128]{1,0:T(8,128)S(1)}, u32[]{:S(2)}, u32[]{:S(2)}) collective-permute-start(f32[24,128]{1,0:T(8,128)S(1)} %get-tuple-element.24), channel_id=1, source_target_pairs={{1,2},{2,1},{5,6},{6,5},{9,10},{10,9},{13,14},{14,13},{17,18},{18,... | collective-permute-start | bytes 36872 | tf_op jit(solution)/shard_map/ppermute | solution.py:25
  29.6 1.8 %collective-permute-done.4.got_a = f32[24,128]{1,0:T(8,128)S(1)} collective-permute-done((f32[24,128]{1,0:T(8,128)S(1)}, f32[24,128]{1,0:T(8,128)S(1)}, u32[]{:S(2)}, u32[]{:S(2)}) %collective-permute-start.4) | collective-permute-done | bytes 12320 | tf_op jit(solution)/shard_map/ppermute | solution.py:25
  31.3 1.9 %collective-permute-done.5.got_b = f32[24,128]{1,0:T(8,128)S(1)} collective-permute-done((f32[24,128]{1,0:T(8,128)S(1)}, f32[24,128]{1,0:T(8,128)S(1)}, u32[]{:S(2)}, u32[]{:S(2)}) %collective-permute-start.5) | collective-permute-done | bytes 12320 | tf_op jit(solution)/shard_map/ppermute | solution.py:25
  33.3 4.0 %step_two.1 = f32[40,16,128]{2,1,0:T(8,128)} custom-call(s32[2]{0:T(128)S(1)} %pad_add_fusion.parity, f32[40,24,128]{2,1,0:T(8,128)S(1)} %get-tuple-element.22.field, f32[49,16,128]{2,1,0:T(8,128)S(1)} %get-tuple-element.15.stencil, f32[24,128]{1,0:T(8,128)S(1)} %collective-permute-done.4.got_a, f32[24,128]{1,0:T(8,128)S(1)} %collective-permute-done.5.got_b), custom_call_target="tpu_custom_call" | custom-call | tf_op jit(solution)/shard_map/step_two/pallas_call | solution.py:252
Async XLA Ops:
  0.0 0.8 %copy-start.3 = (s32[4,16,128]{2,1,0:T(8,128)S(1)}, s32[4,16,128]{2,1,0:T(8,128)}, u32[]{:S(2)}) copy-start(s32[4,16,128]{2,1,0:T(8,128)} %codes.1) | copy-start | bytes 98308
  0.0 0.8 %copy-start.2 = (s32[4,16,128]{2,1,0:T(8,128)S(1)}, s32[4,16,128]{2,1,0:T(8,128)}, u32[]{:S(2)}) copy-start(s32[4,16,128]{2,1,0:T(8,128)} %cells.1) | copy-start | bytes 98308
  0.8 1.0 %copy-start = (f32[40,16,128]{2,1,0:T(8,128)S(1)}, f32[40,16,128]{2,1,0:T(8,128)}, u32[]{:S(2)}) copy-start(f32[40,16,128]{2,1,0:T(8,128)} %mass.3) | copy-start | bytes 983044
  1.7 1.0 %copy-start.1 = (f32[4,10,16,128]{3,2,1,0:T(8,128)S(1)}, f32[4,10,16,128]{3,2,1,0:T(8,128)}, u32[]{:S(2)}) copy-start(f32[4,10,16,128]{3,2,1,0:T(8,128)} %weights.1) | copy-start | bytes 983044
  2.7 0.7 %copy-start.4 = (f32[10,25]{1,0:T(8,128)S(1)}, f32[10,25]{1,0:T(8,128)}, u32[]{:S(2)}) copy-start(f32[10,25]{1,0:T(8,128)} %recon.1) | copy-start | bytes 3004
  5.2 2.6 %collective-permute-start = (f32[392,128]{1,0:T(8,128)S(1)}, f32[392,128]{1,0:T(8,128)S(1)}, u32[]{:S(2)}, u32[]{:S(2)}) collective-permute-start(f32[392,128]{1,0:T(8,128)S(1)} %get-tuple-element.16), channel_id=1, source_target_pairs={{0,4},{4,0},{8,12},{12,8},{16,20},{20,16},{24,28},{28,24},{1,5},{5... | collective-permute-start | bytes 602120 | tf_op jit(solution)/shard_map/ppermute | solution.py:25
  5.3 9.2 %collective-permute-start.1 = (f32[392,128]{1,0:T(8,128)S(1)}, f32[392,128]{1,0:T(8,128)S(1)}, u32[]{:S(2)}, u32[]{:S(2)}) collective-permute-start(f32[392,128]{1,0:T(8,128)S(1)} %get-tuple-element.17), channel_id=1, source_target_pairs={{4,8},{8,4},{12,16},{16,12},{20,24},{24,20},{5,9},{9,5},{13,17},{1... | collective-permute-start | bytes 602120 | tf_op jit(solution)/shard_map/ppermute | solution.py:25
  15.5 3.8 %collective-permute-start.2 = (f32[32,128]{1,0:T(8,128)S(1)}, f32[32,128]{1,0:T(8,128)S(1)}, u32[]{:S(2)}, u32[]{:S(2)}) collective-permute-start(f32[32,128]{1,0:T(8,128)S(1)} %get-tuple-element.20), channel_id=1, source_target_pairs={{0,1},{1,0},{2,3},{3,2},{4,5},{5,4},{6,7},{7,6},{8,9},{9,8},{10,11... | collective-permute-start | bytes 49160 | tf_op jit(solution)/shard_map/ppermute | solution.py:25
  17.1 5.6 %collective-permute-start.3 = (f32[32,128]{1,0:T(8,128)S(1)}, f32[32,128]{1,0:T(8,128)S(1)}, u32[]{:S(2)}, u32[]{:S(2)}) collective-permute-start(f32[32,128]{1,0:T(8,128)S(1)} %get-tuple-element.21), channel_id=1, source_target_pairs={{1,2},{2,1},{5,6},{6,5},{9,10},{10,9},{13,14},{14,13},{17,18},{18,... | collective-permute-start | bytes 49160 | tf_op jit(solution)/shard_map/ppermute | solution.py:25
  27.6 3.8 %collective-permute-start.4 = (f32[24,128]{1,0:T(8,128)S(1)}, f32[24,128]{1,0:T(8,128)S(1)}, u32[]{:S(2)}, u32[]{:S(2)}) collective-permute-start(f32[24,128]{1,0:T(8,128)S(1)} %get-tuple-element.23), channel_id=1, source_target_pairs={{0,1},{1,0},{2,3},{3,2},{4,5},{5,4},{6,7},{7,6},{8,9},{9,8},{10,11... | collective-permute-start | bytes 36872 | tf_op jit(solution)/shard_map/ppermute | solution.py:25
  27.7 5.6 %collective-permute-start.5 = (f32[24,128]{1,0:T(8,128)S(1)}, f32[24,128]{1,0:T(8,128)S(1)}, u32[]{:S(2)}, u32[]{:S(2)}) collective-permute-start(f32[24,128]{1,0:T(8,128)S(1)} %get-tuple-element.24), channel_id=1, source_target_pairs={{1,2},{2,1},{5,6},{6,5},{9,10},{10,9},{13,14},{14,13},{17,18},{18,... | collective-permute-start | bytes 36872 | tf_op jit(solution)/shard_map/ppermute | solution.py:25

commit v2 on v1

--- a/solution.py
+++ b/solution.py
@@ -8,21 +8,29 @@
 from jax.sharding import PartitionSpec as P
 
 F32 = jnp.float32
+ROW_AXES = ("face", "px")
+COLUMN_AXES = "py"
 SWAPPED = (0, 2, 1, 5, 4, 3, 9, 8, 7, 6)
 POWERS = ((0, 0), (1, 0), (0, 1), (2, 0), (1, 1), (0, 2), (3, 0), (2, 1), (1, 2), (0, 3))
 TERMS = 10
 GROUP = 4
 VMEM = pl.BlockSpec(memory_space=pltpu.VMEM)
-SMEM = pl.BlockSpec(memory_space=pltpu.SMEM)
+HBM = pl.BlockSpec(memory_space=pltpu.HBM)
 PARAMS = pltpu.CompilerParams(vmem_limit_bytes=40 * 1024 * 1024)
 
 
 def swap(block, axes, odd_first):
     count = lax.axis_size(axes)
-    pairs = []
+    partner = list(range(count))
     for low in range(1 if odd_first else 0, count - 1, 2):
-        pairs += [(low, low + 1), (low + 1, low)]
+        partner[low], partner[low + 1] = low + 1, low
+    pairs = list(enumerate(partner))
     return lax.ppermute(block, axes, pairs)
+
+
+def position(axes):
+    index = lax.axis_index(axes)
+    return lax.rem(index, 2) == 0, index == 0, index == lax.axis_size(axes) - 1
 
 
 def fill_stencil(recon, weights, cells, codes, turned, spread, stencil, tiles):
@@ -95,10 +103,20 @@
                 stencil[ox * 7 + oy, rows, :] = total[oy]
 
 
-def first_kernel(parity, recon, mass, weights, cells, codes, stencil, send_a, send_b, turned, spread):
+def first_kernel(
+    recon_hbm, mass_hbm, weights_hbm, cells_hbm, codes_hbm, mass, stencil, send_a, send_b,
+    recon, weights, cells, codes, turned, spread, sems,
+):
+    sources = (recon_hbm, codes_hbm, weights_hbm, cells_hbm, mass_hbm)
+    targets = (recon, codes, weights, cells, mass)
+    copies = [pltpu.make_async_copy(a, b, sems.at[i]) for i, (a, b) in enumerate(zip(sources, targets))]
+    for copy in copies:
+        copy.start()
+    for copy in copies:
+        copy.wait()
     fill_stencil(recon, weights, cells, codes, turned, spread, stencil, 2)
     stacks, width = mass.shape[:2]
-    even = parity[0] == 0
+    even = position(ROW_AXES)[0]
     for send, low_edge in ((send_a, jnp.logical_not(even)), (send_b, even)):
         mass_at = jnp.where(low_edge, 0, width - 6)
         stencil_at = jnp.where(low_edge, 0, width - 3)
@@ -109,8 +127,9 @@
             send[at : at + 3, :] = stencil[o, pl.ds(stencil_at, 3), :]
 
 
-def pack_columns(field, tiles, even, send_a, send_b):
+def pack_columns(field, tiles, send_a, send_b):
     stacks = field.shape[0]
+    even = position(COLUMN_AXES)[0]
     lane = lax.broadcasted_iota(jnp.int32, (8, 128), 1)
     for tile in range(tiles):
         rows = pl.ds(8 * tile, 8)
@@ -125,18 +144,18 @@
         send_b[rows, :] = jnp.where(even, left, right)
 
 
-def second_kernel(parity, mass, stencil, got_a, got_b, field, wide, send_a, send_b):
+def second_kernel(mass, stencil, got_a, got_b, field, wide, send_a, send_b):
     stacks, width = mass.shape[:2]
-    even = parity[0] == 0
+    even, first, last = position(ROW_AXES)
 
     def place(above, below):
         for s in range(stacks):
-            field[s, 0:6, :] = above[6 * s : 6 * s + 6, :]
-            field[s, width + 6 : width + 12, :] = below[6 * s : 6 * s + 6, :]
+            field[s, 0:6, :] = jnp.where(first, 0.0, above[6 * s : 6 * s + 6, :])
+            field[s, width + 6 : width + 12, :] = jnp.where(last, 0.0, below[6 * s : 6 * s + 6, :])
         for o in range(49):
             at = 6 * stacks + 3 * o
-            wide[o, 0:3, :] = above[at : at + 3, :]
-            wide[o, width + 3 : width + 6, :] = below[at : at + 3, :]
+            wide[o, 0:3, :] = jnp.where(first, 0.0, above[at : at + 3, :])
+            wide[o, width + 3 : width + 6, :] = jnp.where(last, 0.0, below[at : at + 3, :])
 
     @pl.when(even)
     def _():
@@ -152,11 +171,12 @@
     for o in range(49):
         wide[o, 3 : width + 3, :] = stencil[o, :, :]
         wide[o, width + 6 : width + 8, :] = jnp.zeros((2, 128), F32)
-    pack_columns(field, 4, parity[1] == 0, send_a, send_b)
-
-
-def apply_stencil(even, field, stencil, got_a, got_b, out, shifted, in_tiles, out_tiles):
+    pack_columns(field, 4, send_a, send_b)
+
+
+def apply_stencil(field, stencil, got_a, got_b, out, shifted, in_tiles, out_tiles):
     stacks = field.shape[0]
+    even, first, last = position(COLUMN_AXES)
     lane = lax.broadcasted_iota(jnp.int32, (8, 128), 1)
 
     def some_stacks(group, carry):
@@ -165,8 +185,8 @@
             for tile in range(in_tiles):
                 rows = pl.ds(8 * tile, 8)
                 one, two = got_a[rows, :], got_b[rows, :]
-                after = jnp.where(even, one, two)
-                before = jnp.where(even, two, one)
+                after = jnp.where(last, 0.0, jnp.where(even, one, two))
+                before = jnp.where(first, 0.0, jnp.where(even, two, one))
                 halo = jnp.where(
                     lane < 64,
                     pltpu.roll(after, lax.rem(128 - 3 * s, 128), 1),
@@ -197,67 +217,76 @@
     lax.fori_loop(0, stacks // GROUP, some_stacks, 0)
 
 
-def third_kernel(parity, field, wide, got_a, got_b, out, send_a, send_b, shifted):
-    even = parity[1] == 0
-    apply_stencil(even, field, wide, got_a, got_b, out, shifted, 4, 3)
-    pack_columns(out, 3, even, send_a, send_b)
-
-
-def fourth_kernel(parity, field, stencil, got_a, got_b, out, shifted):
-    apply_stencil(parity[1] == 0, field, stencil, got_a, got_b, out, shifted, 3, 2)
+def third_kernel(field, wide, got_a, got_b, out, send_a, send_b, shifted):
+    apply_stencil(field, wide, got_a, got_b, out, shifted, 4, 3)
+    pack_columns(out, 3, send_a, send_b)
+
+
+def fourth_kernel(field, stencil, got_a, got_b, out, shifted):
+    apply_stencil(field, stencil, got_a, got_b, out, shifted, 3, 2)
 
 
 def local(tracer_mass, recon_table, intersection_weights, intersection_cells, rotation_codes):
     stacks, width_x, width_y = tracer_mass.shape
-    row_axes, column_axes = ("face", "px"), "py"
+    row_axes, column_axes = ROW_AXES, COLUMN_AXES
     shape = lambda *sizes: jax.ShapeDtypeStruct(sizes, F32)
-    parity = jnp.stack([lax.axis_index(row_axes) % 2, lax.axis_index(column_axes) % 2]).astype(jnp.int32)
     edge = -(-(6 * stacks + 3 * 49) // 8) * 8
 
-    stencil, send_a, send_b = pl.pallas_call(
+    mass, stencil, send_a, send_b = pl.pallas_call(
         first_kernel,
-        out_shape=(shape(49, width_x, 128), shape(edge, 128), shape(edge, 128)),
-        in_specs=[SMEM, SMEM, VMEM, VMEM, VMEM, VMEM],
-        out_specs=(VMEM, VMEM, VMEM),
-        scratch_shapes=[pltpu.VMEM((TERMS, 8, 8, 128), F32), pltpu.VMEM((25, 8, 8, 128), F32)],
+        out_shape=(shape(*tracer_mass.shape), shape(49, width_x, 128), shape(edge, 128), shape(edge, 128)),
+        in_specs=[HBM] * 5,
+        out_specs=(VMEM,) * 4,
+        scratch_shapes=[
+            pltpu.SMEM(recon_table.shape, F32),
+            pltpu.VMEM(intersection_weights.shape, F32),
+            pltpu.VMEM(intersection_cells.shape, jnp.int32),
+            pltpu.VMEM(rotation_codes.shape, jnp.int32),
+            pltpu.VMEM((TERMS, 8, 8, 128), F32),
+            pltpu.VMEM((25, 8, 8, 128), F32),
+            pltpu.SemaphoreType.DMA((5,)),
+        ],
         compiler_params=PARAMS,
         name="coefficients",
-    )(parity, recon_table, tracer_mass, intersection_weights, intersection_cells, rotation_codes)
+    )(*(
+        pltpu.with_memory_space_constraint(value, pltpu.HBM)
+        for value in (recon_table, tracer_mass, intersection_weights, intersection_cells, rotation_codes)
+    ))
     got_a = swap(send_a, row_axes, False)
     got_b = swap(send_b, row_axes, True)
 
     field, wide, send_a, send_b = pl.pallas_call(
         second_kernel,
         out_shape=(shape(stacks, 32, 128), shape(49, 24, 128), shape(32, 128), shape(32, 128)),
-        in_specs=[SMEM, VMEM, VMEM, VMEM, VMEM],
+        in_specs=[VMEM] * 4,
         out_specs=(VMEM,) * 4,
         compiler_params=PARAMS,
         name="assemble",
-    )(parity, tracer_mass, stencil, got_a, got_b)
+    )(mass, stencil, got_a, got_b)
     got_a = swap(send_a, column_axes, False)
     got_b = swap(send_b, column_axes, True)
 
     field, send_a, send_b = pl.pallas_call(
         third_kernel,
         out_shape=(shape(stacks, 24, 128), shape(24, 128), shape(24, 128)),
-        in_specs=[SMEM, VMEM, VMEM, VMEM, VMEM],
+        in_specs=[VMEM] * 4,
         out_specs=(VMEM,) * 3,
         scratch_shapes=[pltpu.VMEM((GROUP, 7, 32, 128), F32)],
         compiler_params=PARAMS,
         name="step_one",
-    )(parity, field, wide, got_a, got_b)
+    )(field, wide, got_a, got_b)
     got_a = swap(send_a, column_axes, False)
     got_b = swap(send_b, column_axes, True)
 
     return pl.pallas_call(
         fourth_kernel,
         out_shape=shape(stacks, width_x, 128),
-        in_specs=[SMEM, VMEM, VMEM, VMEM, VMEM],
+        in_specs=[VMEM] * 4,
         out_specs=VMEM,
         scratch_shapes=[pltpu.VMEM((GROUP, 7, 24, 128), F32)],
         compiler_params=PARAMS,
         name="step_two",
-    )(parity, field, stencil, got_a, got_b)
+    )(field, stencil, got_a, got_b)
 
 
 def solution(mesh):

time: 37.6 us -> 33.1 us (0.88)
  the two profiles are of different devices: /device:TPU:20 before, /device:TPU:12 now
where the time goes in v2:
time: 33.1 us; the launch traced here: 32.5 us
  starting transfers between devices  11.7 us (35%)
  Pallas kernels  10.7 us (32%)
  waiting for transfers between devices  10 us (30%)
    ppermute x6, starting transfers between devices, swap(): return lax.ppermute(block, axes, pairs)  11.7 us
    ppermute x6, waiting for transfers between devices, swap(): return lax.ppermute(block, axes, pairs)  10 us
    pallas_call x1, Pallas kernels, local(): pl.pallas_call(third_kernel, out_shape=(shape(stacks, 24, 128), shape(24,...  4.24 us
    pallas_call x1, Pallas kernels, local(): pl.pallas_call(fourth_kernel, out_shape=shape(stacks, width_x, 128), in_s...  3.73 us
    pallas_call x1, Pallas kernels, local(): pl.pallas_call(first_kernel, out_shape=(shape(*tracer_mass.shape), shape(...  2.25 us
  transfers between devices with their start and end apart: 6, of which 3 were waited for; matrix products, arithmetic and copies ran while one was open for 0% of the time, Pallas kernels for 0%

profile of v2, /device:TPU:12, one launch (start us, length us, event | category | flops | bytes accessed | tf_op | source)
XLA Modules:
  0.0 32.5 jit_solution(3639568795756129322)
XLA Ops:
  0.0 2.3 %coefficients.1 = (f32[40,16,128]{2,1,0:T(8,128)S(1)}, f32[49,16,128]{2,1,0:T(8,128)S(1)}, f32[392,128]{1,0:T(8,128)S(1)}, f32[392,128]{1,0:T(8,128)S(1)}) custom-call(f32[10,25]{1,0:T(8,128)} %recon_hbm.1, f32[40,16,128]{2,1,0:T(8,128)} %mass_hbm.1, f32[4,10,16,128]{3,2,1,0:T(8,128)} %weights_hbm.1, s32[4,16,128]{2,1,0:T(8,128)} %cells_hbm.1, ...), custom_call_target="tpu_custom_call" | custom-call | tf_op jit(solution)/shard_map/coefficients/pallas_call | solution.py:235
  2.3 0.1 collective-permute-start
  2.3 2.5 %collective-permute-start.1 = (f32[392,128]{1,0:T(8,128)S(1)}, f32[392,128]{1,0:T(8,128)S(1)}, u32[]{:S(2)}, u32[]{:S(2)}) collective-permute-start(f32[392,128]{1,0:T(8,128)S(1)} %get-tuple-element.19), channel_id=1, source_target_pairs={{0,0},{4,8},{8,4},{12,16},{16,12},{20,24},{24,20},{28,28},{1,1},{5... | collective-permute-start | bytes 602120 | tf_op jit(solution)/shard_map/ppermute | solution.py:28
  4.9 0.0 collective-permute-done.got_a
  4.9 6.7 %collective-permute-done.1.got_b = f32[392,128]{1,0:T(8,128)S(1)} collective-permute-done((f32[392,128]{1,0:T(8,128)S(1)}, f32[392,128]{1,0:T(8,128)S(1)}, u32[]{:S(2)}, u32[]{:S(2)}) %collective-permute-start.1) | collective-permute-done | bytes 200736 | tf_op jit(solution)/shard_map/ppermute | solution.py:28
  11.5 0.5 %assemble.1 = (f32[40,32,128]{2,1,0:T(8,128)S(1)}, f32[49,24,128]{2,1,0:T(8,128)S(1)}, f32[32,128]{1,0:T(8,128)S(1)}, f32[32,128]{1,0:T(8,128)S(1)}) custom-call(f32[40,16,128]{2,1,0:T(8,128)S(1)} %get-tuple-element.16.mass, f32[49,16,128]{2,1,0:T(8,128)S(1)} %get-tuple-element.17.stencil, f32[392,128]{1,0:T(8,128)S(1)} %collective-permute-done.got_a, ...), custom_call_target="tpu_custom_call" | custom-call | tf_op jit(solution)/shard_map/assemble/pallas_call | solution.py:258
  12.1 0.5 %collective-permute-start.2 = (f32[32,128]{1,0:T(8,128)S(1)}, f32[32,128]{1,0:T(8,128)S(1)}, u32[]{:S(2)}, u32[]{:S(2)}) collective-permute-start(f32[32,128]{1,0:T(8,128)S(1)} %get-tuple-element.22), channel_id=1, source_target_pairs={{0,1},{1,0},{2,3},{3,2},{4,5},{5,4},{6,7},{7,6},{8,9},{9,8},{10,11... | collective-permute-start | bytes 49160 | tf_op jit(solution)/shard_map/ppermute | solution.py:28
  12.6 4.6 %collective-permute-start.3 = (f32[32,128]{1,0:T(8,128)S(1)}, f32[32,128]{1,0:T(8,128)S(1)}, u32[]{:S(2)}, u32[]{:S(2)}) collective-permute-start(f32[32,128]{1,0:T(8,128)S(1)} %get-tuple-element.23), channel_id=1, source_target_pairs={{0,0},{1,2},{2,1},{3,3},{4,4},{5,6},{6,5},{7,7},{8,8},{9,10},{10,9... | collective-permute-start | bytes 49160 | tf_op jit(solution)/shard_map/ppermute | solution.py:28
  17.2 0.0 collective-permute-done.2.got_a
  17.2 1.7 %collective-permute-done.3.got_b = f32[32,128]{1,0:T(8,128)S(1)} collective-permute-done((f32[32,128]{1,0:T(8,128)S(1)}, f32[32,128]{1,0:T(8,128)S(1)}, u32[]{:S(2)}, u32[]{:S(2)}) %collective-permute-start.3) | collective-permute-done | bytes 16416 | tf_op jit(solution)/shard_map/ppermute | solution.py:28
  18.9 4.2 %step_one.1 = (f32[40,24,128]{2,1,0:T(8,128)S(1)}, f32[24,128]{1,0:T(8,128)S(1)}, f32[24,128]{1,0:T(8,128)S(1)}) custom-call(f32[40,32,128]{2,1,0:T(8,128)S(1)} %get-tuple-element.20.field, f32[49,24,128]{2,1,0:T(8,128)S(1)} %get-tuple-element.21.wide, f32[32,128]{1,0:T(8,128)S(1)} %collective-permute-done.2.got_a, f32[32,128]{1,0:T(8,128)S(1)} %collective-permute-done.3.got_b), custom_call_target="tpu_custom_call" | custom-call | tf_op jit(solution)/shard_map/step_one/pallas_call | solution.py:269
  23.1 0.1 collective-permute-start.4
  23.2 3.9 %collective-permute-start.5 = (f32[24,128]{1,0:T(8,128)S(1)}, f32[24,128]{1,0:T(8,128)S(1)}, u32[]{:S(2)}, u32[]{:S(2)}) collective-permute-start(f32[24,128]{1,0:T(8,128)S(1)} %get-tuple-element.26), channel_id=1, source_target_pairs={{0,0},{1,2},{2,1},{3,3},{4,4},{5,6},{6,5},{7,7},{8,8},{9,10},{10,9... | collective-permute-start | bytes 36872 | tf_op jit(solution)/shard_map/ppermute | solution.py:28
  27.1 0.0 collective-permute-done.4.got_a
  27.1 1.6 %collective-permute-done.5.got_b = f32[24,128]{1,0:T(8,128)S(1)} collective-permute-done((f32[24,128]{1,0:T(8,128)S(1)}, f32[24,128]{1,0:T(8,128)S(1)}, u32[]{:S(2)}, u32[]{:S(2)}) %collective-permute-start.5) | collective-permute-done | bytes 12320 | tf_op jit(solution)/shard_map/ppermute | solution.py:28
  28.8 3.7 %step_two.1 = f32[40,16,128]{2,1,0:T(8,128)} custom-call(f32[40,24,128]{2,1,0:T(8,128)S(1)} %get-tuple-element.24.field, f32[49,16,128]{2,1,0:T(8,128)S(1)} %get-tuple-element.17.stencil, f32[24,128]{1,0:T(8,128)S(1)} %collective-permute-done.4.got_a, f32[24,128]{1,0:T(8,128)S(1)} %collective-permute-done.5.got_b), custom_call_target="tpu_custom_call" | custom-call | tf_op jit(solution)/shard_map/step_two/pallas_call | solution.py:281
Async XLA Ops:
  2.3 2.6 %collective-permute-start = (f32[392,128]{1,0:T(8,128)S(1)}, f32[392,128]{1,0:T(8,128)S(1)}, u32[]{:S(2)}, u32[]{:S(2)}) collective-permute-start(f32[392,128]{1,0:T(8,128)S(1)} %get-tuple-element.18), channel_id=1, source_target_pairs={{0,4},{4,0},{8,12},{12,8},{16,20},{20,16},{24,28},{28,24},{1,5},{5... | collective-permute-start | bytes 602120 | tf_op jit(solution)/shard_map/ppermute | solution.py:28
  2.3 9.2 %collective-permute-start.1 = (f32[392,128]{1,0:T(8,128)S(1)}, f32[392,128]{1,0:T(8,128)S(1)}, u32[]{:S(2)}, u32[]{:S(2)}) collective-permute-start(f32[392,128]{1,0:T(8,128)S(1)} %get-tuple-element.19), channel_id=1, source_target_pairs={{0,0},{4,8},{8,4},{12,16},{16,12},{20,24},{24,20},{28,28},{1,1},{5... | collective-permute-start | bytes 602120 | tf_op jit(solution)/shard_map/ppermute | solution.py:28
  12.1 5.1 %collective-permute-start.2 = (f32[32,128]{1,0:T(8,128)S(1)}, f32[32,128]{1,0:T(8,128)S(1)}, u32[]{:S(2)}, u32[]{:S(2)}) collective-permute-start(f32[32,128]{1,0:T(8,128)S(1)} %get-tuple-element.22), channel_id=1, source_target_pairs={{0,1},{1,0},{2,3},{3,2},{4,5},{5,4},{6,7},{7,6},{8,9},{9,8},{10,11... | collective-permute-start | bytes 49160 | tf_op jit(solution)/shard_map/ppermute | solution.py:28
  12.6 6.3 %collective-permute-start.3 = (f32[32,128]{1,0:T(8,128)S(1)}, f32[32,128]{1,0:T(8,128)S(1)}, u32[]{:S(2)}, u32[]{:S(2)}) collective-permute-start(f32[32,128]{1,0:T(8,128)S(1)} %get-tuple-element.23), channel_id=1, source_target_pairs={{0,0},{1,2},{2,1},{3,3},{4,4},{5,6},{6,5},{7,7},{8,8},{9,10},{10,9... | collective-permute-start | bytes 49160 | tf_op jit(solution)/shard_map/ppermute | solution.py:28
  23.1 4.0 %collective-permute-start.4 = (f32[24,128]{1,0:T(8,128)S(1)}, f32[24,128]{1,0:T(8,128)S(1)}, u32[]{:S(2)}, u32[]{:S(2)}) collective-permute-start(f32[24,128]{1,0:T(8,128)S(1)} %get-tuple-element.25), channel_id=1, source_target_pairs={{0,1},{1,0},{2,3},{3,2},{4,5},{5,4},{6,7},{7,6},{8,9},{9,8},{10,11... | collective-permute-start | bytes 36872 | tf_op jit(solution)/shard_map/ppermute | solution.py:28
  23.2 5.6 %collective-permute-start.5 = (f32[24,128]{1,0:T(8,128)S(1)}, f32[24,128]{1,0:T(8,128)S(1)}, u32[]{:S(2)}, u32[]{:S(2)}) collective-permute-start(f32[24,128]{1,0:T(8,128)S(1)} %get-tuple-element.26), channel_id=1, source_target_pairs={{0,0},{1,2},{2,1},{3,3},{4,4},{5,6},{6,5},{7,7},{8,8},{9,10},{10,9... | collective-permute-start | bytes 36872 | tf_op jit(solution)/shard_map/ppermute | solution.py:28

commit v3 on v2

--- a/solution.py
+++ b/solution.py
@@ -127,9 +127,9 @@
             send[at : at + 3, :] = stencil[o, pl.ds(stencil_at, 3), :]
 
 
-def pack_columns(field, tiles, send_a, send_b):
+def pack_columns(field, tiles, send):
     stacks = field.shape[0]
-    even = position(COLUMN_AXES)[0]
+    here_at = lax.axis_index(COLUMN_AXES)
     lane = lax.broadcasted_iota(jnp.int32, (8, 128), 1)
     for tile in range(tiles):
         rows = pl.ds(8 * tile, 8)
@@ -140,11 +140,13 @@
             value = field[s, rows, :]
             left = jnp.where(here, pltpu.roll(value, (3 * s) % 128, 1), left)
             right = jnp.where(here, pltpu.roll(value, (3 * s - 125) % 128, 1), right)
-        send_a[rows, :] = jnp.where(even, right, left)
-        send_b[rows, :] = jnp.where(even, left, right)
-
-
-def second_kernel(mass, stencil, got_a, got_b, field, wide, send_a, send_b):
+        for target in range(send.shape[0]):
+            send[target, rows, :] = jnp.where(
+                target == here_at + 1, right, jnp.where(target == here_at - 1, left, 0.0)
+            )
+
+
+def second_kernel(mass, stencil, got_a, got_b, field, wide, send):
     stacks, width = mass.shape[:2]
     even, first, last = position(ROW_AXES)
 
@@ -171,12 +173,15 @@
     for o in range(49):
         wide[o, 3 : width + 3, :] = stencil[o, :, :]
         wide[o, width + 6 : width + 8, :] = jnp.zeros((2, 128), F32)
-    pack_columns(field, 4, send_a, send_b)
-
-
-def apply_stencil(field, stencil, got_a, got_b, out, shifted, in_tiles, out_tiles):
+    pack_columns(field, 4, send)
+
+
+def apply_stencil(field, stencil, got, out, shifted, in_tiles, out_tiles):
     stacks = field.shape[0]
-    even, first, last = position(COLUMN_AXES)
+    _, first, last = position(COLUMN_AXES)
+    here_at = lax.axis_index(COLUMN_AXES)
+    after_at = jnp.where(last, 0, here_at + 1)
+    before_at = jnp.where(first, 0, here_at - 1)
     lane = lax.broadcasted_iota(jnp.int32, (8, 128), 1)
 
     def some_stacks(group, carry):
@@ -184,9 +189,8 @@
             s = group * GROUP + k
             for tile in range(in_tiles):
                 rows = pl.ds(8 * tile, 8)
-                one, two = got_a[rows, :], got_b[rows, :]
-                after = jnp.where(last, 0.0, jnp.where(even, one, two))
-                before = jnp.where(first, 0.0, jnp.where(even, two, one))
+                after = jnp.where(last, 0.0, got[after_at, rows, :])
+                before = jnp.where(first, 0.0, got[before_at, rows, :])
                 halo = jnp.where(
                     lane < 64,
                     pltpu.roll(after, lax.rem(128 - 3 * s, 128), 1),
@@ -217,13 +221,13 @@
     lax.fori_loop(0, stacks // GROUP, some_stacks, 0)
 
 
-def third_kernel(field, wide, got_a, got_b, out, send_a, send_b, shifted):
-    apply_stencil(field, wide, got_a, got_b, out, shifted, 4, 3)
-    pack_columns(out, 3, send_a, send_b)
-
-
-def fourth_kernel(field, stencil, got_a, got_b, out, shifted):
-    apply_stencil(field, stencil, got_a, got_b, out, shifted, 3, 2)
+def third_kernel(field, wide, got, out, send, shifted):
+    apply_stencil(field, wide, got, out, shifted, 4, 3)
+    pack_columns(out, 3, send)
+
+
+def fourth_kernel(field, stencil, got, out, shifted):
+    apply_stencil(field, stencil, got, out, shifted, 3, 2)
 
 
 def local(tracer_mass, recon_table, intersection_weights, intersection_cells, rotation_codes):
@@ -255,38 +259,37 @@
     got_a = swap(send_a, row_axes, False)
     got_b = swap(send_b, row_axes, True)
 
-    field, wide, send_a, send_b = pl.pallas_call(
+    across = lax.axis_size(column_axes)
+    field, wide, send = pl.pallas_call(
         second_kernel,
-        out_shape=(shape(stacks, 32, 128), shape(49, 24, 128), shape(32, 128), shape(32, 128)),
+        out_shape=(shape(stacks, 32, 128), shape(49, 24, 128), shape(across, 32, 128)),
         in_specs=[VMEM] * 4,
-        out_specs=(VMEM,) * 4,
+        out_specs=(VMEM,) * 3,
         compiler_params=PARAMS,
         name="assemble",
     )(mass, stencil, got_a, got_b)
-    got_a = swap(send_a, column_axes, False)
-    got_b = swap(send_b, column_axes, True)
-
-    field, send_a, send_b = pl.pallas_call(
+    got = lax.all_to_all(send, column_axes, 0, 0, tiled=True)
+
+    field, send = pl.pallas_call(
         third_kernel,
-        out_shape=(shape(stacks, 24, 128), shape(24, 128), shape(24, 128)),
-        in_specs=[VMEM] * 4,
-        out_specs=(VMEM,) * 3,
+        out_shape=(shape(stacks, 24, 128), shape(across, 24, 128)),
+        in_specs=[VMEM] * 3,
+        out_specs=(VMEM,) * 2,
         scratch_shapes=[pltpu.VMEM((GROUP, 7, 32, 128), F32)],
         compiler_params=PARAMS,
         name="step_one",
-    )(field, wide, got_a, got_b)
-    got_a = swap(send_a, column_axes, False)
-    got_b = swap(send_b, column_axes, True)
+    )(field, wide, got)
+    got = lax.all_to_all(send, column_axes, 0, 0, tiled=True)
 
     return pl.pallas_call(
         fourth_kernel,
         out_shape=shape(stacks, width_x, 128),
-        in_specs=[VMEM] * 4,
+        in_specs=[VMEM] * 3,
         out_specs=VMEM,
         scratch_shapes=[pltpu.VMEM((GROUP, 7, 24, 128), F32)],
         compiler_params=PARAMS,
         name="step_two",
-    )(field, stencil, got_a, got_b)
+    )(field, stencil, got)
 
 
 def solution(mesh):

time: 33.1 us -> 38.8 us (1.17)
  the two profiles are of different devices: /device:TPU:12 before, /device:TPU:4 now
where the time goes in v3:
time: 38.8 us; the launch traced here: 38.5 us
  blocking collectives  18.5 us (48%)
  Pallas kernels  10.8 us (28%)
  waiting for transfers between devices  7.25 us (19%)
  starting transfers between devices  1.99 us (5%)
    all_to_all x2, blocking collectives, local(): got = lax.all_to_all(send, column_axes, 0, 0, tiled=True)  18.5 us
    ppermute x2, waiting for transfers between devices, swap(): return lax.ppermute(block, axes, pairs)  7.25 us
    pallas_call x1, Pallas kernels, local(): pl.pallas_call(third_kernel, out_shape=(shape(stacks, 24, 128), shape(acr...  4.22 us
    pallas_call x1, Pallas kernels, local(): pl.pallas_call(fourth_kernel, out_shape=shape(stacks, width_x, 128), in_s...  3.76 us
    pallas_call x1, Pallas kernels, local(): pl.pallas_call(first_kernel, out_shape=(shape(*tracer_mass.shape), shape(...  2.25 us
    ppermute x2, starting transfers between devices, swap(): return lax.ppermute(block, axes, pairs)  1.99 us
  transfers between devices with their start and end apart: 2, of which 1 were waited for; matrix products, arithmetic and copies ran while one was open for 0% of the time, Pallas kernels for 0%

profile of v3, /device:TPU:4, one launch (start us, length us, event | category | flops | bytes accessed | tf_op | source)
XLA Modules:
  0.0 38.5 jit_solution(12772930635951065022)
XLA Ops:
  0.0 2.3 %coefficients.1 = (f32[40,16,128]{2,1,0:T(8,128)S(1)}, f32[49,16,128]{2,1,0:T(8,128)S(1)}, f32[392,128]{1,0:T(8,128)S(1)}, f32[392,128]{1,0:T(8,128)S(1)}) custom-call(f32[10,25]{1,0:T(8,128)} %recon_hbm.1, f32[40,16,128]{2,1,0:T(8,128)} %mass_hbm.1, f32[4,10,16,128]{3,2,1,0:T(8,128)} %weights_hbm.1, s32[4,16,128]{2,1,0:T(8,128)} %cells_hbm.1, ...), custom_call_target="tpu_custom_call" | custom-call | tf_op jit(solution)/shard_map/coefficients/pallas_call | solution.py:239
  2.3 0.1 collective-permute-start
  2.3 1.9 %collective-permute-start.1 = (f32[392,128]{1,0:T(8,128)S(1)}, f32[392,128]{1,0:T(8,128)S(1)}, u32[]{:S(2)}, u32[]{:S(2)}) collective-permute-start(f32[392,128]{1,0:T(8,128)S(1)} %get-tuple-element.17), channel_id=1, source_target_pairs={{0,0},{4,8},{8,4},{12,16},{16,12},{20,24},{24,20},{28,28},{1,1},{5... | collective-permute-start | bytes 602120 | tf_op jit(solution)/shard_map/ppermute | solution.py:28
  4.3 0.0 collective-permute-done.got_a
  4.3 7.2 %collective-permute-done.1.got_b = f32[392,128]{1,0:T(8,128)S(1)} collective-permute-done((f32[392,128]{1,0:T(8,128)S(1)}, f32[392,128]{1,0:T(8,128)S(1)}, u32[]{:S(2)}, u32[]{:S(2)}) %collective-permute-start.1) | collective-permute-done | bytes 200736 | tf_op jit(solution)/shard_map/ppermute | solution.py:28
  11.5 0.5 %assemble.1 = (f32[40,32,128]{2,1,0:T(8,128)S(1)}, f32[49,24,128]{2,1,0:T(8,128)S(1)}, f32[4,32,128]{2,1,0:T(8,128)S(1)}) custom-call(f32[40,16,128]{2,1,0:T(8,128)S(1)} %get-tuple-element.14.mass, f32[49,16,128]{2,1,0:T(8,128)S(1)} %get-tuple-element.15.stencil, f32[392,128]{1,0:T(8,128)S(1)} %collective-permute-done.got_a, ...), custom_call_target="tpu_custom_call" | custom-call | tf_op jit(solution)/shard_map/assemble/pallas_call | solution.py:263
  12.1 10.4 %all_to_all.10.got = f32[4,32,128]{2,1,0:T(8,128)S(1)} all-to-all(f32[4,32,128]{2,1,0:T(8,128)S(1)} %get-tuple-element.20), channel_id=1, replica_groups=mesh['face'=2,'px'=4,'py'=4] {'py'}, dimensions={0} | all-to-all | bytes 131072 | tf_op jit(solution)/shard_map/all_to_all | solution.py:271
  22.5 4.2 %step_one.1 = (f32[40,24,128]{2,1,0:T(8,128)S(1)}, f32[4,24,128]{2,1,0:T(8,128)S(1)}) custom-call(f32[40,32,128]{2,1,0:T(8,128)S(1)} %get-tuple-element.18.field, f32[49,24,128]{2,1,0:T(8,128)S(1)} %get-tuple-element.19.wide, f32[4,32,128]{2,1,0:T(8,128)S(1)} %all_to_all.10.got), custom_call_target="tpu_custom_call" | custom-call | tf_op jit(solution)/shard_map/step_one/pallas_call | solution.py:273
  26.7 8.1 %all_to_all.11.got = f32[4,24,128]{2,1,0:T(8,128)S(1)} all-to-all(f32[4,24,128]{2,1,0:T(8,128)S(1)} %get-tuple-element.22), channel_id=1, replica_groups=mesh['face'=2,'px'=4,'py'=4] {'py'}, dimensions={0} | all-to-all | bytes 98304 | tf_op jit(solution)/shard_map/all_to_all | solution.py:282
  34.8 3.8 %step_two.1 = f32[40,16,128]{2,1,0:T(8,128)} custom-call(f32[40,24,128]{2,1,0:T(8,128)S(1)} %get-tuple-element.21.field, f32[49,16,128]{2,1,0:T(8,128)S(1)} %get-tuple-element.15.stencil, f32[4,24,128]{2,1,0:T(8,128)S(1)} %all_to_all.11.got), custom_call_target="tpu_custom_call" | custom-call | tf_op jit(solution)/shard_map/step_two/pallas_call | solution.py:284
Async XLA Ops:
  2.3 2.0 %collective-permute-start = (f32[392,128]{1,0:T(8,128)S(1)}, f32[392,128]{1,0:T(8,128)S(1)}, u32[]{:S(2)}, u32[]{:S(2)}) collective-permute-start(f32[392,128]{1,0:T(8,128)S(1)} %get-tuple-element.16), channel_id=1, source_target_pairs={{0,4},{4,0},{8,12},{12,8},{16,20},{20,16},{24,28},{28,24},{1,5},{5... | collective-permute-start | bytes 602120 | tf_op jit(solution)/shard_map/ppermute | solution.py:28
  2.3 9.2 %collective-permute-start.1 = (f32[392,128]{1,0:T(8,128)S(1)}, f32[392,128]{1,0:T(8,128)S(1)}, u32[]{:S(2)}, u32[]{:S(2)}) collective-permute-start(f32[392,128]{1,0:T(8,128)S(1)} %get-tuple-element.17), channel_id=1, source_target_pairs={{0,0},{4,8},{8,4},{12,16},{16,12},{20,24},{24,20},{28,28},{1,1},{5... | collective-permute-start | bytes 602120 | tf_op jit(solution)/shard_map/ppermute | solution.py:28
